TPU v7x, 32 devices: a whole 2x2x4 slice. The times are simulated.
32 devices in a mesh: row: 8 (over z, core), col: 4 (over y, x).
Axes of the slice: x: 2, y: 2, z: 4, core: 2. Of those that a mesh axis runs over, the one named last changes fastest.
Arguments:
- inputs: bfloat16 [3, 64, 64, 512], P(None, None, 'row', 'col'), may hold values from -6 to 6
- gate_pre: bfloat16 [3, 256, 64, 512], P(None, None, 'row', 'col'), may hold values from -8 to 8
- cotangent: bfloat16 [3, 64, 64, 512], P(None, None, 'row', 'col'), may hold values from -6 to 6
- hidden_init: bfloat16 [64, 64, 512], P(None, 'row', 'col'), may hold values from -6 to 6
- cell_init: float32 [64, 64, 512], P(None, 'row', 'col'), may hold values from -6 to 6
- land_mask: int32 [64, 512], P('row', 'col'), may hold values 0 or 1
- kernel: bfloat16 [256, 1152], replicated, may hold values from -0.1875 to 0.1875
Outputs:
- grad_inputs: bfloat16 [3, 64, 64, 512], P(None, None, 'row', 'col')
- grad_hidden: float32 [64, 64, 512], P(None, 'row', 'col')
- grad_cell: float32 [64, 64, 512], P(None, 'row', 'col')
- grad_kernel: float32 [256, 1152], P('row', 'col')
- grad_bias: float32 [256], P(('row', 'col'))
Inputs may be any that keep to these rules, and one draw needn't show every extreme that they name: `land_mask`: 1 marks a land cell.
All inputs are finite; a program needn't handle non-finite values. No bound on the sum of `land_mask` on one device may be relied on, other than what follows from the above.
Results may differ from a plain program's by a relative error of at most 0.005.
Values may be sent and summed in bfloat16 or wider, within the bound.
A program may use at most 64 MiB of HBM per device.

v0:
```python
import math

import jax
import jax.numpy as jnp
from jax import lax
from jax.sharding import PartitionSpec as P


def with_halo(block, sides, width):
    for axis, dim in sides:
        count = lax.axis_size(axis)
        forward = [(i, i + 1) for i in range(count - 1)]
        backward = [(target, source) for source, target in forward]
        low = lax.ppermute(
            lax.slice_in_dim(block, block.shape[dim] - width, None, axis=dim), axis, forward
        )
        high = lax.ppermute(lax.slice_in_dim(block, 0, width, axis=dim), axis, backward)
        block = jnp.concatenate([low, block, high], axis=dim)
    return block


def gate_parts(pre, hidden):
    return (
        jax.nn.sigmoid(pre[:hidden]),
        jax.nn.sigmoid(pre[hidden : 2 * hidden]),
        jax.nn.sigmoid(pre[2 * hidden : 3 * hidden]),
        jnp.tanh(pre[3 * hidden :]),
    )


def kernel_terms(grads, padded, rows, cols):
    flat = grads.reshape(grads.shape[0], rows * cols)
    blocks = []
    for offset in range(9):
        upper, left = (offset // 3, offset % 3)
        window = padded[:, upper : upper + rows, left : left + cols].reshape(
            padded.shape[0], rows * cols
        )
        blocks.append(
            lax.dot_general(
                flat, window, (((1,), (1,)), ((), ())), preferred_element_type=jnp.float32
            )
        )
    return jnp.concatenate(blocks, axis=1)


def transposed(kernel, padded_grads, rows, cols, width):
    total = jnp.zeros((width, rows * cols), jnp.float32)
    for offset in range(9):
        upper, left = (offset // 3, offset % 3)
        window = padded_grads[:, 2 - upper : 2 - upper + rows, 2 - left : 2 - left + cols]
        window = window.reshape(padded_grads.shape[0], rows * cols)
        piece = kernel[:, offset * width : (offset + 1) * width]
        total = total + lax.dot_general(
            piece, window, (((0,), (0,)), ((), ())), preferred_element_type=jnp.float32
        )
    return total


def reduce_grads(kernel_part, bias_part):
    row_kernel, row_bias = (
        lax.psum_scatter(kernel_part, "row", scatter_dimension=0, tiled=True),
        lax.psum_scatter(bias_part, "row", scatter_dimension=0, tiled=True),
    )
    return (
        lax.psum_scatter(row_kernel, "col", scatter_dimension=1, tiled=True),
        lax.psum_scatter(row_bias, "col", scatter_dimension=0, tiled=True),
    )


def shards(inputs, gate_pre, cotangent, hidden_init, cell_init, land_mask, kernel):
    steps = inputs.shape[0]
    width_in = inputs.shape[1]
    hidden = hidden_init.shape[0]
    width = width_in + hidden
    rows, cols = land_mask.shape
    mask = land_mask.astype(jnp.float32)
    scale = 1.0 / math.sqrt(rows * cols * lax.axis_size("row") * lax.axis_size("col"))
    states = [cell_init]
    layers = []
    hidden_now = hidden_init
    acts = []
    for step in range(steps):
        gates = gate_parts(gate_pre[step].astype(jnp.float32), hidden)
        acts.append(gates)
        layers.append(jnp.concatenate([inputs[step], hidden_now], axis=0))
        new_cell = gates[1] * states[-1] + gates[0] * gates[3]
        states.append(new_cell)
        hidden_now = (mask * gates[2] * jnp.tanh(new_cell)).astype(jnp.bfloat16)
    padded_all = with_halo(jnp.stack(layers), (("row", 2), ("col", 3)), 1)
    grad_h = jnp.zeros((hidden, rows, cols), jnp.float32)
    grad_c = jnp.zeros((hidden, rows, cols), jnp.float32)
    kernel_total = None
    bias_total = None
    outs = [None] * steps
    for step in reversed(range(steps)):
        gin, gfor, gout, gcand = acts[step]
        tanh_cell = jnp.tanh(states[step + 1])
        error = mask * (grad_h + cotangent[step].astype(jnp.float32))
        grad_c = grad_c + error * gout * (1.0 - tanh_cell * tanh_cell)
        grads = jnp.concatenate(
            [
                grad_c * gcand * gin * (1.0 - gin),
                grad_c * states[step] * gfor * (1.0 - gfor),
                error * tanh_cell * gout * (1.0 - gout),
                grad_c * gin * (1.0 - gcand * gcand),
            ],
            axis=0,
        ).astype(jnp.bfloat16)
        grad_c = grad_c * gfor
        padded_grads = with_halo(grads, (("row", 1), ("col", 2)), 1)
        kernel_part = scale * kernel_terms(grads, padded_all[step], rows, cols)
        bias_part = scale * jnp.sum(grads.astype(jnp.float32), axis=(1, 2))
        reduced_kernel, reduced_bias = reduce_grads(kernel_part, bias_part)
        if kernel_total is None:
            kernel_total, bias_total = (reduced_kernel, reduced_bias)
        else:
            kernel_total = kernel_total + reduced_kernel
            bias_total = bias_total + reduced_bias
        back = transposed(kernel, padded_grads, rows, cols, width)
        outs[step] = back[:width_in].reshape(width_in, rows, cols).astype(jnp.bfloat16)
        grad_h = back[width_in:].reshape(hidden, rows, cols)
    return (jnp.stack(outs), grad_h, grad_c, kernel_total, bias_total)


def solution(mesh):
    placed = (
        P(None, None, "row", "col"),
        P(None, None, "row", "col"),
        P(None, None, "row", "col"),
        P(None, "row", "col"),
        P(None, "row", "col"),
        P("row", "col"),
        P(),
    )
    return jax.shard_map(
        shards,
        mesh=mesh,
        in_specs=placed,
        out_specs=(
            P(None, None, "row", "col"),
            P(None, "row", "col"),
            P(None, "row", "col"),
            P("row", "col"),
            P(("row", "col")),
        ),
        check_vma=False,
    )
```

profile of v0, /device:TPU:0, one launch (start us, length us, event | category | flops | bytes accessed | tf_op | source)
XLA Modules:
  0.0 259.1 jit_solution(10364431143986211559)
XLA Ops:
  15.3 3.0 %collective-permute-start = (bf16[256,1,128]{2,0,1:T(8,128)(2,1)}, bf16[256,1,128]{2,0,1:T(8,128)(2,1)S(1)}, u32[]{:S(2)}, u32[]{:S(2)}) collective-permute-start(bf16[256,1,128]{2,0,1:T(8,128)(2,1)} %get-tuple-element.97), channel_id=1, source_target_pairs={{0,4},{4,8},{8,12},{12,16},{16,20},{20,24},{24,28},{1,5},{5,9},{9,... | collective-permute-start | bytes 196616 | tf_op jit(solution)/shard_map/ppermute | solution.py:14
  20.7 5.8 %collective-permute-start.12 = (bf16[3,128,1,128]{3,1,2,0:T(8,128)(2,1)}, bf16[3,128,1,128]{3,1,2,0:T(8,128)(2,1)}, u32[]{:S(2)}, u32[]{:S(2)}) collective-permute-start(bf16[3,128,1,128]{3,1,2,0:T(8,128)(2,1)} %get-tuple-element.73), channel_id=1, source_target_pairs={{0,4},{4,8},{8,12},{12,16},{16,20},{20,24},{24,28},{1,5},{5,9},{9,... | collective-permute-start | bytes 294920 | tf_op jit(solution)/shard_map/ppermute | solution.py:14
  37.9 5.1 %collective-permute-start.3 = (bf16[256,10,1]{0,1,2:T(8,128)(2,1)}, bf16[256,10,1]{0,1,2:T(8,128)(2,1)}, u32[]{:S(2)}, u32[]{:S(2)}) collective-permute-start(bf16[256,10,1]{0,1,2:T(8,128)(2,1)} %copy.89), channel_id=1, source_target_pairs={{0,1},{1,2},{2,3},{4,5},{5,6},{6,7},{8,9},{9,10},{10,11},{12,13},{... | collective-permute-start | bytes 15368 | tf_op jit(solution)/shard_map/ppermute | solution.py:14
  46.2 2.1 fusion.153
  54.1 4.1 %pad_maximum_fusion.1 = (bf16[256,10,129]{2,0,1:T(8,128)(2,1)}, bf16[256,10,129]{2,0,1:T(8,128)(2,1)S(1)}) fusion(bf16[256,10,1]{2,0,1:T(8,128)(2,1)} %copy.86, bf16[256,1,128]{2,0,1:T(8,128)(2,1)S(1)} %collective-permute-done.1, bf16[64,8,128]{2,0,1:T(8,128)(2,1)S(1)} %get-tuple-element.69, bf16[64,8,128]{2,0,1:T(8,128)(2,1)S(1)} %get-tuple-element.70, ...), kind=kLoop, calls=%fused_computation.1 | loop fusion | flops 9246720 | bytes 1986560 | tf_op jit(solution)/shard_map/concatenate | solution.py:18
  60.6 3.6 %fusion.172 = (bf16[256,8,128]{2,0,1:T(8,128)(2,1)}, bf16[256,8,128]{2,0,1:T(8,128)(2,1)}, bf16[256,8,128]{2,0,1:T(8,128)(2,1)}) fusion(bf16[256,10,129]{2,0,1:T(8,128)(2,1)} %get-tuple-element.83), kind=kLoop, calls=%fused_computation.332 | loop fusion | bytes 3145728 | tf_op jit(solution)/shard_map/slice | solution.py:51
  64.2 2.1 copy.87
  66.3 2.2 fusion.159
  68.5 2.1 copy.92
  93.0 2.3 copy.142
  95.2 5.1 %collective-permute-start.14 = (bf16[3,128,10,1]{1,0,3,2:T(4,128)(2,1)}, bf16[3,128,10,1]{1,0,3,2:T(4,128)(2,1)}, u32[]{:S(2)}, u32[]{:S(2)}) collective-permute-start(bf16[3,128,10,1]{1,0,3,2:T(4,128)(2,1)} %copy.142), channel_id=1, source_target_pairs={{0,1},{1,2},{2,3},{4,5},{5,6},{6,7},{8,9},{9,10},{10,11},{12,13},{... | collective-permute-start | bytes 23048 | tf_op jit(solution)/shard_map/ppermute | solution.py:14
  102.3 3.0 %collective-permute-start.4 = (bf16[256,1,128]{2,0,1:T(8,128)(2,1)S(1)}, bf16[256,1,128]{2,0,1:T(8,128)(2,1)S(1)}, u32[]{:S(2)}, u32[]{:S(2)}) collective-permute-start(bf16[256,1,128]{2,0,1:T(8,128)(2,1)S(1)} %get-tuple-element.93), channel_id=1, source_target_pairs={{0,4},{4,8},{8,12},{12,16},{16,20},{20,24},{24,28},{1,5},{5,9},{9,... | collective-permute-start | bytes 196616 | tf_op jit(solution)/shard_map/ppermute | solution.py:14
  107.4 2.1 copy.144
  109.5 3.6 %pad_maximum_fusion = bf16[3,128,10,130]{3,1,2,0:T(8,128)(2,1)S(1)} fusion(bf16[3,128,10,1]{3,1,2,0:T(8,128)(2,1)} %copy.145, bf16[3,128,1,128]{3,1,2,0:T(8,128)(2,1)} %collective-permute-done.13, bf16[1,128,8,128]{3,1,2,0:T(8,128)(2,1)S(1)} %copy-done.13, bf16[1,128,8,128]{3,1,2,0:T(8,128)(2,1)S(1)} %copy-done.15, bf16[1,128,8,128]{3,1,2,0:T(8,128)(2,1)} %copy-done.16, ...), kind=kLoop, calls=%fused_computation | loop fusion | flops 6988800 | bytes 1996800 | tf_op jit(solution)/shard_map/concatenate | solution.py:18
  125.1 4.9 %collective-permute-start.7 = (bf16[256,10,1]{0,1,2:T(8,128)(2,1)}, bf16[256,10,1]{0,1,2:T(8,128)(2,1)S(1)}, u32[]{:S(2)}, u32[]{:S(2)}) collective-permute-start(bf16[256,10,1]{0,1,2:T(8,128)(2,1)} %copy.107), channel_id=1, source_target_pairs={{0,1},{1,2},{2,3},{4,5},{5,6},{6,7},{8,9},{9,10},{10,11},{12,13},{... | collective-permute-start | bytes 15368 | tf_op jit(solution)/shard_map/ppermute | solution.py:14
  136.5 3.0 %pad_maximum_fusion.2 = (bf16[256,10,129]{2,0,1:T(8,128)(2,1)S(1)}, bf16[256,10,129]{2,0,1:T(8,128)(2,1)S(1)}) fusion(bf16[256,10,1]{2,0,1:T(8,128)(2,1)} %copy.104, bf16[256,1,128]{2,0,1:T(8,128)(2,1)} %copy-done.43, bf16[64,8,128]{2,0,1:T(8,128)(2,1)S(1)} %copy-done.9, bf16[64,8,128]{2,0,1:T(8,128)(2,1)S(1)} %copy-done.5, ...), kind=kLoop, calls=%fused_computation.3 | loop fusion | flops 9246720 | bytes 1986560 | tf_op jit(solution)/shard_map/concatenate | solution.py:18
  148.3 2.1 copy.116
  150.4 2.1 copy.118
  163.6 3.5 %collective-permute-start.8 = (bf16[256,1,128]{2,0,1:T(8,128)(2,1)S(1)}, bf16[256,1,128]{2,0,1:T(8,128)(2,1)S(1)}, u32[]{:S(2)}, u32[]{:S(2)}) collective-permute-start(bf16[256,1,128]{2,0,1:T(8,128)(2,1)S(1)} %get-tuple-element.89), channel_id=1, source_target_pairs={{0,4},{4,8},{8,12},{12,16},{16,20},{20,24},{24,28},{1,5},{5,9},{9,... | collective-permute-start | bytes 196616 | tf_op jit(solution)/shard_map/ppermute | solution.py:14
  173.3 15.3 %all-reduce = f32[256]{0:T(256)S(1)} all-reduce(f32[256]{0:T(256)S(1)} %add_multiply_fusion.1), channel_id=12, replica_groups=mesh['row'=8,'col'=4] {'row'}, use_global_device_ids=true, to_apply=%region_7.0.clone | all-reduce | flops 256 | bytes 2048
  188.7 10.5 %all-reduce.1 = f32[32]{0:T(128)S(1)} all-reduce(f32[32]{0:T(128)S(1)} %dynamic-slice.1), channel_id=13, replica_groups=mesh['row'=8,'col'=4] {'col'}, use_global_device_ids=true, to_apply=%region_8.0.clone | all-reduce | flops 32 | bytes 256
  204.1 4.8 %collective-permute-start.11 = (bf16[256,10,1]{0,1,2:T(8,128)(2,1)S(1)}, bf16[256,10,1]{0,1,2:T(8,128)(2,1)S(1)}, u32[]{:S(2)}, u32[]{:S(2)}) collective-permute-start(bf16[256,10,1]{0,1,2:T(8,128)(2,1)S(1)} %copy.126), channel_id=1, source_target_pairs={{0,1},{1,2},{2,3},{4,5},{5,6},{6,7},{8,9},{9,10},{10,11},{12,13},{... | collective-permute-start | bytes 15368 | tf_op jit(solution)/shard_map/ppermute | solution.py:14
  211.3 2.2 pad_maximum_fusion.3
  229.1 21.6 %reduce-scatter.5.cloned.1.call-done = f32[32,288]{0,1:T(8,128)} async-done(((f32[32,1152]{0,1:T(8,128)}), f32[32,288]{0,1:T(8,128)}) %reduce-scatter.5.cloned.1.call-update) | async-done | bytes 36880 | tf_op jit(solution)/shard_map/reduce_scatter | solution.py:66
  (328 shorter events, 126.0 us)
Async XLA Ops:
  7.2 218.3 %reduce-scatter.7.cloned.1.call-start = ((), (), s32[]{:S(2)}) async-start(), calls=%async_computation.3 | async-start | bytes 1327104
  11.6 71.7 %copy-start.18 = (f32[64,8,128]{2,0,1:T(8,128)}, f32[64,8,128]{2,0,1:T(8,128)S(1)}, u32[]{:S(2)}) copy-start(f32[64,8,128]{2,0,1:T(8,128)S(1)} %get-tuple-element.27) | copy-start | bytes 786436
  14.1 17.6 %collective-permute-start.1 = (bf16[256,1,128]{2,0,1:T(8,128)(2,1)}, bf16[256,1,128]{2,0,1:T(8,128)(2,1)S(1)}, u32[]{:S(2)}, u32[]{:S(2)}) collective-permute-start(bf16[256,1,128]{2,0,1:T(8,128)(2,1)} %get-tuple-element.98), channel_id=1, source_target_pairs={{4,0},{8,4},{12,8},{16,12},{20,16},{24,20},{28,24},{5,1},{9,5},{13... | collective-permute-start | bytes 196616 | tf_op jit(solution)/shard_map/ppermute | solution.py:17
  15.3 16.3 %collective-permute-start = (bf16[256,1,128]{2,0,1:T(8,128)(2,1)}, bf16[256,1,128]{2,0,1:T(8,128)(2,1)S(1)}, u32[]{:S(2)}, u32[]{:S(2)}) collective-permute-start(bf16[256,1,128]{2,0,1:T(8,128)(2,1)} %get-tuple-element.97), channel_id=1, source_target_pairs={{0,4},{4,8},{8,12},{12,16},{16,20},{20,24},{24,28},{1,5},{5,9},{9,... | collective-permute-start | bytes 196616 | tf_op jit(solution)/shard_map/ppermute | solution.py:14
  18.6 11.8 %copy-start.67 = (u32[32]{0:T(128)S(1)}, u32[32]{0:T(128)}, u32[]{:S(2)}) copy-start(u32[32]{0:T(128)} %constant.13) | copy-start | bytes 388
  19.4 67.7 %collective-permute-start.13 = (bf16[3,128,1,128]{3,1,2,0:T(8,128)(2,1)}, bf16[3,128,1,128]{3,1,2,0:T(8,128)(2,1)}, u32[]{:S(2)}, u32[]{:S(2)}) collective-permute-start(bf16[3,128,1,128]{3,1,2,0:T(8,128)(2,1)} %get-tuple-element.74), channel_id=1, source_target_pairs={{4,0},{8,4},{12,8},{16,12},{20,16},{24,20},{28,24},{5,1},{9,5},{13... | collective-permute-start | bytes 294920 | tf_op jit(solution)/shard_map/ppermute | solution.py:17
  20.7 66.5 %collective-permute-start.12 = (bf16[3,128,1,128]{3,1,2,0:T(8,128)(2,1)}, bf16[3,128,1,128]{3,1,2,0:T(8,128)(2,1)}, u32[]{:S(2)}, u32[]{:S(2)}) collective-permute-start(bf16[3,128,1,128]{3,1,2,0:T(8,128)(2,1)} %get-tuple-element.73), channel_id=1, source_target_pairs={{0,4},{4,8},{8,12},{12,16},{16,20},{20,24},{24,28},{1,5},{5,9},{9,... | collective-permute-start | bytes 294920 | tf_op jit(solution)/shard_map/ppermute | solution.py:14
  34.5 15.9 %collective-permute-start.2 = (bf16[256,10,1]{0,1,2:T(8,128)(2,1)S(1)}, bf16[256,10,1]{0,1,2:T(8,128)(2,1)}, u32[]{:S(2)}, u32[]{:S(2)}) collective-permute-start(bf16[256,10,1]{0,1,2:T(8,128)(2,1)S(1)} %copy.85), channel_id=1, source_target_pairs={{1,0},{2,1},{3,2},{5,4},{6,5},{7,6},{9,8},{10,9},{11,10},{13,12},{... | collective-permute-start | bytes 15368 | tf_op jit(solution)/shard_map/ppermute | solution.py:17
  37.9 14.4 %collective-permute-start.3 = (bf16[256,10,1]{0,1,2:T(8,128)(2,1)}, bf16[256,10,1]{0,1,2:T(8,128)(2,1)}, u32[]{:S(2)}, u32[]{:S(2)}) collective-permute-start(bf16[256,10,1]{0,1,2:T(8,128)(2,1)} %copy.89), channel_id=1, source_target_pairs={{0,1},{1,2},{2,3},{4,5},{5,6},{6,7},{8,9},{9,10},{10,11},{12,13},{... | collective-permute-start | bytes 15368 | tf_op jit(solution)/shard_map/ppermute | solution.py:14
  83.4 46.6 %copy-start.2 = (bf16[64,8,128]{2,0,1:T(8,128)(2,1)}, bf16[64,8,128]{2,0,1:T(8,128)(2,1)S(1)}, u32[]{:S(2)}) copy-start(bf16[64,8,128]{2,0,1:T(8,128)(2,1)S(1)} %get-tuple-element.32) | copy-start | bytes 393220
  83.4 46.6 %copy-start.4 = (bf16[64,8,128]{2,0,1:T(8,128)(2,1)}, bf16[64,8,128]{2,0,1:T(8,128)(2,1)S(1)}, u32[]{:S(2)}) copy-start(bf16[64,8,128]{2,0,1:T(8,128)(2,1)S(1)} %get-tuple-element.41) | copy-start | bytes 393220
  83.6 46.4 %copy-start.6 = (bf16[64,8,128]{2,0,1:T(8,128)(2,1)}, bf16[64,8,128]{2,0,1:T(8,128)(2,1)S(1)}, u32[]{:S(2)}) copy-start(bf16[64,8,128]{2,0,1:T(8,128)(2,1)S(1)} %get-tuple-element.60) | copy-start | bytes 393220
  83.6 46.4 %copy-start.8 = (bf16[64,8,128]{2,0,1:T(8,128)(2,1)}, bf16[64,8,128]{2,0,1:T(8,128)(2,1)S(1)}, u32[]{:S(2)}) copy-start(bf16[64,8,128]{2,0,1:T(8,128)(2,1)S(1)} %get-tuple-element.61) | copy-start | bytes 393220
  91.7 13.7 %collective-permute-start.15 = (bf16[3,128,10,1]{1,0,3,2:T(4,128)(2,1)S(1)}, bf16[3,128,10,1]{1,0,3,2:T(4,128)(2,1)}, u32[]{:S(2)}, u32[]{:S(2)}) collective-permute-start(bf16[3,128,10,1]{1,0,3,2:T(4,128)(2,1)S(1)} %copy.143), channel_id=1, source_target_pairs={{1,0},{2,1},{3,2},{5,4},{6,5},{7,6},{9,8},{10,9},{11,10},{13,12},{... | collective-permute-start | bytes 23048 | tf_op jit(solution)/shard_map/ppermute | solution.py:17
  95.2 12.2 %collective-permute-start.14 = (bf16[3,128,10,1]{1,0,3,2:T(4,128)(2,1)}, bf16[3,128,10,1]{1,0,3,2:T(4,128)(2,1)}, u32[]{:S(2)}, u32[]{:S(2)}) collective-permute-start(bf16[3,128,10,1]{1,0,3,2:T(4,128)(2,1)} %copy.142), channel_id=1, source_target_pairs={{0,1},{1,2},{2,3},{4,5},{5,6},{6,7},{8,9},{9,10},{10,11},{12,13},{... | collective-permute-start | bytes 23048 | tf_op jit(solution)/shard_map/ppermute | solution.py:14
  101.0 18.2 %collective-permute-start.5 = (bf16[256,1,128]{2,0,1:T(8,128)(2,1)S(1)}, bf16[256,1,128]{2,0,1:T(8,128)(2,1)S(1)}, u32[]{:S(2)}, u32[]{:S(2)}) collective-permute-start(bf16[256,1,128]{2,0,1:T(8,128)(2,1)S(1)} %get-tuple-element.94), channel_id=1, source_target_pairs={{4,0},{8,4},{12,8},{16,12},{20,16},{24,20},{28,24},{5,1},{9,5},{13... | collective-permute-start | bytes 196616 | tf_op jit(solution)/shard_map/ppermute | solution.py:17
  102.3 17.9 %collective-permute-start.4 = (bf16[256,1,128]{2,0,1:T(8,128)(2,1)S(1)}, bf16[256,1,128]{2,0,1:T(8,128)(2,1)S(1)}, u32[]{:S(2)}, u32[]{:S(2)}) collective-permute-start(bf16[256,1,128]{2,0,1:T(8,128)(2,1)S(1)} %get-tuple-element.93), channel_id=1, source_target_pairs={{0,4},{4,8},{8,12},{12,16},{16,20},{20,24},{24,28},{1,5},{5,9},{9,... | collective-permute-start | bytes 196616 | tf_op jit(solution)/shard_map/ppermute | solution.py:14
  122.8 10.6 %collective-permute-start.6 = (bf16[256,10,1]{0,1,2:T(8,128)(2,1)S(1)}, bf16[256,10,1]{0,1,2:T(8,128)(2,1)}, u32[]{:S(2)}, u32[]{:S(2)}) collective-permute-start(bf16[256,10,1]{0,1,2:T(8,128)(2,1)S(1)} %copy.103), channel_id=1, source_target_pairs={{1,0},{2,1},{3,2},{5,4},{6,5},{7,6},{9,8},{10,9},{11,10},{13,12},{... | collective-permute-start | bytes 15368 | tf_op jit(solution)/shard_map/ppermute | solution.py:17
  125.1 10.2 %collective-permute-start.7 = (bf16[256,10,1]{0,1,2:T(8,128)(2,1)}, bf16[256,10,1]{0,1,2:T(8,128)(2,1)S(1)}, u32[]{:S(2)}, u32[]{:S(2)}) collective-permute-start(bf16[256,10,1]{0,1,2:T(8,128)(2,1)} %copy.107), channel_id=1, source_target_pairs={{0,1},{1,2},{2,3},{4,5},{5,6},{6,7},{8,9},{9,10},{10,11},{12,13},{... | collective-permute-start | bytes 15368 | tf_op jit(solution)/shard_map/ppermute | solution.py:14
  162.3 37.5 %collective-permute-start.9 = (bf16[256,1,128]{2,0,1:T(8,128)(2,1)S(1)}, bf16[256,1,128]{2,0,1:T(8,128)(2,1)S(1)}, u32[]{:S(2)}, u32[]{:S(2)}) collective-permute-start(bf16[256,1,128]{2,0,1:T(8,128)(2,1)S(1)} %get-tuple-element.90), channel_id=1, source_target_pairs={{4,0},{8,4},{12,8},{16,12},{20,16},{24,20},{28,24},{5,1},{9,5},{13... | collective-permute-start | bytes 196616 | tf_op jit(solution)/shard_map/ppermute | solution.py:17
  163.6 36.2 %collective-permute-start.8 = (bf16[256,1,128]{2,0,1:T(8,128)(2,1)S(1)}, bf16[256,1,128]{2,0,1:T(8,128)(2,1)S(1)}, u32[]{:S(2)}, u32[]{:S(2)}) collective-permute-start(bf16[256,1,128]{2,0,1:T(8,128)(2,1)S(1)} %get-tuple-element.89), channel_id=1, source_target_pairs={{0,4},{4,8},{8,12},{12,16},{16,20},{20,24},{24,28},{1,5},{5,9},{9,... | collective-permute-start | bytes 196616 | tf_op jit(solution)/shard_map/ppermute | solution.py:14
  173.2 77.5 %reduce-scatter.5.cloned.1.call-start = ((), (), s32[]{:S(2)}) async-start(), calls=%async_computation.2 | async-start | bytes 737280 | tf_op jit(solution)/shard_map/reduce_scatter | solution.py:66
  202.4 8.2 %collective-permute-start.10 = (bf16[256,10,1]{0,1,2:T(8,128)(2,1)S(1)}, bf16[256,10,1]{0,1,2:T(8,128)(2,1)S(1)}, u32[]{:S(2)}, u32[]{:S(2)}) collective-permute-start(bf16[256,10,1]{0,1,2:T(8,128)(2,1)S(1)} %copy.122), channel_id=1, source_target_pairs={{1,0},{2,1},{3,2},{5,4},{6,5},{7,6},{9,8},{10,9},{11,10},{13,12},{... | collective-permute-start | bytes 15368 | tf_op jit(solution)/shard_map/ppermute | solution.py:17
  204.1 6.9 %collective-permute-start.11 = (bf16[256,10,1]{0,1,2:T(8,128)(2,1)S(1)}, bf16[256,10,1]{0,1,2:T(8,128)(2,1)S(1)}, u32[]{:S(2)}, u32[]{:S(2)}) collective-permute-start(bf16[256,10,1]{0,1,2:T(8,128)(2,1)S(1)} %copy.126), channel_id=1, source_target_pairs={{0,1},{1,2},{2,3},{4,5},{5,6},{6,7},{8,9},{9,10},{10,11},{12,13},{... | collective-permute-start | bytes 15368 | tf_op jit(solution)/shard_map/ppermute | solution.py:14
  (63 other events, 177.1 us)
Sparse Core Ops, SparseCore 0:
  173.3 34.8 reduce-scatter.6
  227.6 23.0 reduce-scatter.4
where the time goes:
time: 261 us; the launch traced here: 259 us
  local copies, waits for them, and re-layouts  98.9 us (38%)
  starting transfers between devices  45.6 us (17%)
  matrix products  28.6 us (11%)
  blocking collectives  25.8 us (10%)
  other arithmetic  21.7 us (8%)
  waiting for transfers between devices  21.7 us (8%)
  between operations  16.9 us (6%)
    slice x30, local copies, waits for them, and re-layouts, transposed(): padded_grads[:, 2 - upper:2 - upper + rows, 2 - left:2 - left + cols]  40.4 us
    ppermute x8, starting transfers between devices, with_halo(): lax.ppermute(lax.slice_in_dim(block, block.shape[dim] - width, None, axis...  35.2 us
    unnamed x2, blocking collectives  25.8 us
    reduce_scatter x1, waiting for transfers between devices, reduce_grads(): lax.psum_scatter(row_kernel, 'col', scatter_dimension=1, tiled=True)  21.6 us
    dot_general x27, matrix products, transposed(): lax.dot_general(piece, window, (((0,), (0,)), ((), ())), preferred_elemen...  20 us
    unnamed x156, local copies, waits for them, and re-layouts  18.8 us
    concatenate x11, other arithmetic, with_halo(): block = jnp.concatenate([low, block, high], axis=dim)  15.7 us
    ppermute x8, starting transfers between devices, with_halo(): lax.ppermute(lax.slice_in_dim(block, 0, width, axis=dim), axis, backward)  10.3 us
  transfers between devices with their start and end apart: 18, of which 1 were waited for; matrix products, arithmetic and copies ran while one was open for 39% of the time, Pallas kernels for 0%

commit v1 on v0

v1 whole, which is shorter than its diff:
```python
import functools
import math

import jax
import jax.numpy as jnp
from jax import lax
from jax.experimental import pallas as pl
from jax.experimental.pallas import tpu as pltpu
from jax.sharding import PartitionSpec as P

MESH = pl.DeviceIdType.MESH
F32 = jnp.float32
BF16 = jnp.bfloat16
SIDES = ((-1, 0), (1, 0), (0, 1), (1, 1), (-1, 1), (0, -1), (1, -1), (-1, -1))
BLOCK = 16


def nt(lhs, rhs):
    return lax.dot_general(lhs, rhs, (((1,), (1,)), ((), ())), preferred_element_type=F32)


def nn(lhs, rhs):
    return jnp.dot(lhs, rhs, preferred_element_type=F32)


def sigmoid(value):
    return 0.5 * jnp.tanh(0.5 * value) + 0.5


def body(
    dims,
    inp_in, pre_in, cot_in, hid_in, cell_in, mask_in, weight_in,
    gin_hbm, gh_hbm, gc_hbm, gk_hbm, bias_hbm,
    inp, pre, cot, hid, cell, mask, weight, load_sem,
    acts, cells, tanhs, gradc, nat, zst, aall, edges, border, shifter, weight_t, selector,
    product, kacc, kfull, kown, kbuf, r1, s1own, s1, r2, s2own, s2, r3,
    send_sem, recv_sem, rs_send, rs_recv,
    gin_out, gh_out, gc_out, gk_out, bias_out, store_sem,
):
    steps, cin, hidden, rows, cols, nrow, ncol = dims
    width = cin + hidden
    gates = 4 * hidden
    padded = (rows + 2) * cols
    edge = edges.shape[2]
    half = nrow // 2
    high = gates // nrow
    part = weight.shape[1] // ncol
    lanes = kbuf.shape[-1]
    row, col = lax.axis_index("row"), lax.axis_index("col")
    zpos, core = row // 2, row % 2
    scale = 1.0 / math.sqrt(rows * cols * nrow * ncol)

    def inside(r, c):
        return (r >= 0) & (r < nrow) & (c >= 0) & (c < ncol)

    loads = [pltpu.make_async_copy(pre_in.at[step], pre.at[step], load_sem.at[step]) for step in range(steps)]
    for n, (source, target) in enumerate(
        ((cell_in, cell), (mask_in, mask), (weight_in, weight), (cot_in, cot), (inp_in, inp), (hid_in, hid))
    ):
        loads.append(pltpu.make_async_copy(source, target, load_sem.at[steps + n]))
    for n in (0, steps, steps + 1, steps + 2, *range(1, steps), steps + 3, steps + 4, steps + 5):
        loads[n].start()

    border[...] = jnp.zeros_like(border)
    for step in range(steps):
        aall[step, gates : 2 * gates, 0:cols] = jnp.zeros((gates, cols), BF16)
        aall[step, gates : 2 * gates, padded - cols : padded] = jnp.zeros((gates, cols), BF16)

    barrier = pltpu.get_barrier_semaphore()
    for dr, dc in SIDES:
        @pl.when(inside(row + dr, col + dc))
        def _():
            pl.semaphore_signal(barrier, inc=1, device_id=(row + dr, col + dc), device_id_type=MESH)
    sibling = row + 1 - 2 * core
    pl.semaphore_signal(barrier, inc=1, device_id=(sibling, col), device_id_type=MESH)
    for j in range(1, ncol):
        pl.semaphore_signal(barrier, inc=1, device_id=(row, (col + j) % ncol), device_id_type=MESH)
    for j in range(1, half):
        pl.semaphore_signal(barrier, inc=1, device_id=(((zpos + j) % half) * 2 + core, col), device_id_type=MESH)

    srow = lax.broadcasted_iota(jnp.int32, (2 * cols, 2 * cols), 0)
    scol = lax.broadcasted_iota(jnp.int32, (2 * cols, 2 * cols), 1)
    for j in range(rows + 2):
        if j == 0:
            low, up = edge + rows - 1, 4 * edge + rows - 1
        elif j == rows + 1:
            low, up = 2 * edge, 5 * edge
        else:
            low, up = j - 1, 3 * edge + j - 1
        source = jnp.where(
            scol < cols,
            jnp.where(scol == 0, cols + low, scol - 1),
            jnp.where(scol == 2 * cols - 1, cols + up, scol - cols + 1),
        )
        shifter[j] = (srow == source).astype(F32).astype(BF16)
    prow = lax.broadcasted_iota(jnp.int32, selector.shape, 0)
    pcol = lax.broadcasted_iota(jnp.int32, selector.shape, 1)
    wanted = jnp.where(prow < edge, prow * cols, (prow - edge) * cols + cols - 1)
    valid = (prow % edge) < rows
    selector[...] = ((pcol == wanted) & valid).astype(F32).astype(BF16)
    irow = lax.broadcasted_iota(jnp.int32, (gates, gates), 0)
    icol = lax.broadcasted_iota(jnp.int32, (gates, gates), 1)
    identity = (irow == icol).astype(F32).astype(BF16)

    loads[0].wait()
    loads[steps].wait()
    loads[steps + 1].wait()
    land = mask[...].astype(F32)[None]
    cells[0] = cell[...]
    gradc[...] = jnp.zeros_like(gradc)

    def place_z(step, first, count):
        for r in range(rows):
            tile = nat[pl.ds(r, count, stride=rows), :].astype(BF16)
            for dr in range(3):
                at = (r + 2 - dr) * cols
                zst[step, dr * width + first : dr * width + first + count, at : at + cols] = tile

    for step in range(steps):
        for dr in range(3):
            for i in range(rows + 2):
                if not 0 <= i + dr - 2 < rows:
                    zst[step, dr * width : (dr + 1) * width, i * cols : (i + 1) * cols] = jnp.zeros((width, cols), BF16)

    def spread(ref, step=None):
        def put(b, carry):
            at = pl.ds(b * BLOCK, BLOCK)
            value = (ref[at] if step is None else ref[step, at]).astype(F32)
            nat[pl.ds(b * BLOCK * rows, BLOCK * rows), :] = value.reshape(BLOCK * rows, cols)
            return carry
        lax.fori_loop(0, ref.shape[-3] // BLOCK, put, 0)

    for step in range(steps):
        if step:
            loads[step].wait()

        def forward(b, carry):
            def gate(n):
                return pre[step, pl.ds(n * hidden + b * BLOCK, BLOCK)].astype(F32)
            at = pl.ds(b * BLOCK, BLOCK)
            gi, gf, go, gg = sigmoid(gate(0)), sigmoid(gate(1)), sigmoid(gate(2)), jnp.tanh(gate(3))
            new = gf * cells[step, at] + gi * gg
            tn = jnp.tanh(new)
            acts[step, 0, at] = gi
            acts[step, 1, at] = gf
            acts[step, 2, at] = go
            acts[step, 3, at] = gg
            cells[step + 1, at] = new
            tanhs[step, at] = tn
            nat[pl.ds(b * BLOCK * rows, BLOCK * rows), :] = (land * go * tn).reshape(BLOCK * rows, cols)
            return carry
        lax.fori_loop(0, hidden // BLOCK, forward, 0)
        if step + 1 < steps:
            place_z(step + 1, cin, hidden)

    loads[steps + 3].wait()

    def halo(step, d):
        dr, dc = SIDES[d]
        if dc == 0:
            first = cols if dr < 0 else rows * cols
            land_at = padded - cols if dr < 0 else 0
            src = aall.at[step, pl.ds(gates, gates), pl.ds(first, cols)]
            dst = aall.at[step, pl.ds(gates, gates), pl.ds(land_at, cols)]
        else:
            src = edges.at[step, 1 if dc > 0 else 0]
            dst = border.at[step, pl.ds((d - 2) * edge, edge)]
        return pltpu.make_async_remote_copy(
            src_ref=src, dst_ref=dst, send_sem=send_sem.at[step, d], recv_sem=recv_sem.at[step, d],
            device_id=(row + dr, col + dc), device_id_type=MESH,
        )

    def start_halo(step):
        for d, (dr, dc) in enumerate(SIDES):
            @pl.when(inside(row + dr, col + dc))
            def _():
                halo(step, d).start()

    def wait_halo(step):
        for d, (dr, dc) in enumerate(SIDES):
            @pl.when(inside(row - dr, col - dc))
            def _():
                halo(step, d).wait_recv()

    def wait_sent(step):
        for d, (dr, dc) in enumerate(SIDES):
            @pl.when(inside(row + dr, col + dc))
            def _():
                halo(step, d).wait_send()

    def kernel_terms(step):
        term = nt(aall[step], zst[step])
        kacc[...] = term if step == steps - 1 else kacc[...] + term

    def emit_inputs(step):
        def put(b, carry):
            at = pl.ds(b * BLOCK, BLOCK)
            gin_out[step, at] = nat[pl.ds((gates + b * BLOCK) * rows, BLOCK * rows), :].reshape(BLOCK, rows, cols).astype(BF16)
            return carry
        lax.fori_loop(0, cin // BLOCK, put, 0)
        store = pltpu.make_async_copy(gin_out.at[step], gin_hbm.at[step], store_sem.at[step])
        store.start()
        stores.append(store)

    def transposed(step):
        product[...] = nn(weight_t[...], aall[step])
        for r in range(rows):
            total = None
            for dr in range(3):
                at = (r + 2 - dr) * cols
                piece = product[dr * width : (dr + 1) * width, at : at + cols]
                total = piece if total is None else total + piece
            gxn = pl.ds(gates * rows + r, cin, stride=rows)
            nat[gxn, :] = total[:cin]
            dhn = pl.ds((gates + cin) * rows + r, hidden, stride=rows)
            nat[dhn, :] = total[cin:]

    bias = None
    stores = []
    for step in reversed(range(steps)):
        last = step == steps - 1

        def backward(b, carry):
            at = pl.ds(b * BLOCK, BLOCK)
            gi, gf, go, gg = (acts[step, n, at] for n in range(4))
            tn = tanhs[step, at]
            err = cot[step, at].astype(F32)
            if not last:
                err = err + nat[pl.ds((gates + cin + b * BLOCK) * rows, BLOCK * rows), :].reshape(BLOCK, rows, cols)
            err = land * err
            dc = gradc[at] + err * go * (1.0 - tn * tn)
            dci = dc * gi
            dcf = dc * gf
            parts = (
                dci * gg * (1.0 - gi),
                dcf * cells[step, at] * (1.0 - gf),
                err * tn * go * (1.0 - go),
                dci * (1.0 - gg * gg),
            )
            for n, value in enumerate(parts):
                nat[pl.ds((n * hidden + b * BLOCK) * rows, BLOCK * rows), :] = value.reshape(BLOCK * rows, cols)
            gradc[at] = dcf
            return carry
        lax.fori_loop(0, hidden // BLOCK, backward, 0)
        for r in range(rows):
            tile = nat[pl.ds(r, gates, stride=rows), :].astype(BF16)
            aall[step, gates : 2 * gates, (r + 1) * cols : (r + 2) * cols] = tile
            bias = tile.astype(F32) if last and r == 0 else bias + tile.astype(F32)
        own = aall[step, gates : 2 * gates, cols : padded - cols]
        picked = nt(selector[...], own).astype(BF16)
        edges[step, 0] = picked[:edge]
        edges[step, 1] = picked[edge:]
        if last:
            pl.semaphore_wait(barrier, number_of_partners(row, col, nrow, ncol, inside))
        start_halo(step)
        if last:
            loads[steps + 2].wait()
            for dr in range(3):
                for dc in range(3):
                    k = 3 * dr + dc
                    weight_t[dr * width : (dr + 1) * width, dc * gates : (dc + 1) * gates] = (
                        weight[:, k * width : (k + 1) * width].astype(F32).T.astype(BF16)
                    )
            loads[steps + 4].wait()
            loads[steps + 5].wait()
            spread(hid)
            place_z(0, cin, hidden)
            for s in range(steps):
                spread(inp, s)
                place_z(s, 0, cin)
        else:
            emit_inputs(step + 1)
            kernel_terms(step + 1)
        wait_halo(step)
        side = nt(identity, border[step]).astype(BF16)
        for j in range(rows + 2):
            at = slice(j * cols, (j + 1) * cols)
            pair = jnp.concatenate([aall[step, gates : 2 * gates, at], side], axis=1)
            moved = nn(pair, shifter[j]).astype(BF16)
            aall[step, 2 * gates : 3 * gates, at] = moved[:, :cols]
            aall[step, 0:gates, at] = moved[:, cols:]
        if step > 0:
            transposed(step)
        wait_sent(step)

    kernel_terms(0)
    for dr in range(3):
        for dc in range(3):
            k = 3 * dr + dc
            kfull[:, k * width : (k + 1) * width] = kacc[dc * gates : (dc + 1) * gates, dr * width : (dr + 1) * width] * scale
    lane = lax.broadcasted_iota(jnp.int32, (gates, lanes), 1)
    tail = lanes - 128

    def split(value):
        block = value[..., tail:]
        at = lax.broadcasted_iota(jnp.int32, block.shape, block.ndim - 1) + tail
        whole = jnp.where(at == part, block + pltpu.roll(block, 127, block.ndim - 1), block)
        own = jnp.where(at == part + 1, 0.0, whole)
        lost = pltpu.roll(own - own.astype(BF16).astype(F32), 1, block.ndim - 1)
        sent = jnp.where(at == part + 1, lost, own).astype(BF16)
        if not tail:
            return own, sent
        rest = value[..., :tail]
        return (
            jnp.concatenate([rest, own], axis=-1),
            jnp.concatenate([rest.astype(BF16), sent], axis=-1),
        )

    bias = jnp.sum(bias, axis=1, keepdims=True) * scale
    for c in range(ncol):
        base, shift = part * c // 128 * 128, part * c % 128
        piece = kfull[:, base : base + lanes + 128]
        if shift:
            piece = pltpu.roll(piece, lanes + 128 - shift, 1)
        piece = jnp.where(lane < part, piece[:, :lanes], jnp.where(lane == part, bias, 0.0))
        sent = split(piece)[1]
        for r in range(nrow):
            kown[r % 2, c, r // 2] = piece[r * high : (r + 1) * high]
            kbuf[r % 2, c, r // 2] = sent[r * high : (r + 1) * high]

    def first():
        return pltpu.make_async_remote_copy(
            src_ref=kbuf.at[1 - core], dst_ref=r1, send_sem=rs_send.at[0], recv_sem=rs_recv.at[0],
            device_id=(sibling, col), device_id_type=MESH,
        )

    def second(j):
        to = (col + j) % ncol
        return pltpu.make_async_remote_copy(
            src_ref=s1.at[to], dst_ref=r2.at[j - 1], send_sem=rs_send.at[j], recv_sem=rs_recv.at[j],
            device_id=(row, to), device_id_type=MESH,
        )

    def third(j):
        to = (zpos + j) % half
        return pltpu.make_async_remote_copy(
            src_ref=s2.at[to], dst_ref=r3.at[j - 1], send_sem=rs_send.at[ncol + j], recv_sem=rs_recv.at[ncol + j],
            device_id=(to * 2 + core, col), device_id_type=MESH,
        )

    first().start()
    transposed(0)
    first().wait_recv()
    for c in range(ncol):
        for z in range(half):
            s1own[c, z], s1[c, z] = split(kown[core, c, z] + r1[c, z].astype(F32))
    for j in range(1, ncol):
        second(j).start()
    emit_inputs(0)
    gh_out[...] = nat[pl.ds((gates + cin) * rows, hidden * rows), :].reshape(hidden, rows, cols)
    gc_out[...] = gradc[...]
    for n, (source, target) in enumerate(((gh_out, gh_hbm), (gc_out, gc_hbm))):
        store = pltpu.make_async_copy(source, target, store_sem.at[steps + n])
        store.start()
        stores.append(store)
    for j in range(1, ncol):
        second(j).wait_recv()
    for z in range(half):
        total = s1own[col, z]
        for j in range(1, ncol):
            total = total + r2[j - 1, z].astype(F32)
        s2own[z], s2[z] = split(total)
    for j in range(1, half):
        third(j).start()
    total = s2own[zpos]
    for j in range(1, half):
        third(j).wait_recv()
        total = total + r3[j - 1].astype(F32)
    gk_out[...] = total[:, :part]
    block = total[:, tail:]
    line = lax.broadcasted_iota(jnp.int32, block.shape, 0)
    lane = lax.broadcasted_iota(jnp.int32, block.shape, 1)
    column = jnp.sum(jnp.where((lane == part - tail) | (lane == part + 1 - tail), block, 0.0), axis=1, keepdims=True)
    each = high // ncol
    wanted = line == lane + col * each
    bias_out[...] = jnp.sum(jnp.where(wanted, column, 0.0), axis=0, keepdims=True)[:, :each]
    for n, (source, target) in enumerate(((gk_out, gk_hbm), (bias_out, bias_hbm))):
        store = pltpu.make_async_copy(source, target, store_sem.at[steps + 2 + n])
        store.start()
        stores.append(store)
    for store in stores:
        store.wait()
    first().wait_send()
    for j in range(1, ncol):
        second(j).wait_send()
    for j in range(1, half):
        third(j).wait_send()


def number_of_partners(row, col, nrow, ncol, inside):
    count = jnp.int32(1 + (ncol - 1) + (nrow // 2 - 1))
    for dr, dc in SIDES:
        count = count + inside(row + dr, col + dc).astype(jnp.int32)
    return count


def finish(*refs):
    sem = refs[-1]
    count = (len(refs) - 1) // 2
    copies = [pltpu.make_async_copy(refs[n], refs[count + n], sem.at[n]) for n in range(count)]
    for copy in copies:
        copy.start()
    for copy in copies:
        copy.wait()


def shards(nrow, ncol, inputs, gate_pre, cotangent, hidden_init, cell_init, land_mask, kernel):
    steps, cin = inputs.shape[:2]
    hidden = hidden_init.shape[0]
    rows, cols = land_mask.shape
    width, gates = cin + hidden, 4 * hidden
    taps = kernel.shape[1]
    padded = (rows + 2) * cols
    edge = -(-rows // 16) * 16
    half, high, part = nrow // 2, gates // nrow, taps // ncol
    lanes = ((part + 1) // 128 + 1) * 128
    plane = (hidden, rows, cols)
    slots = max(half - 1, 1)
    scratch = [
        pltpu.VMEM(inputs.shape, BF16),
        pltpu.VMEM(gate_pre.shape, BF16),
        pltpu.VMEM(cotangent.shape, BF16),
        pltpu.VMEM(plane, BF16),
        pltpu.VMEM(plane, F32),
        pltpu.VMEM((rows, cols), jnp.int32),
        pltpu.VMEM(kernel.shape, BF16),
        pltpu.SemaphoreType.DMA((steps + 6,)),
        pltpu.VMEM((steps, 4) + plane, F32),
        pltpu.VMEM((steps + 1,) + plane, F32),
        pltpu.VMEM((steps,) + plane, F32),
        pltpu.VMEM(plane, F32),
        pltpu.VMEM(((gates + width) * rows, cols), F32),
        pltpu.VMEM((steps, 3 * width, padded), BF16),
        pltpu.VMEM((steps, 3 * gates, padded), BF16),
        pltpu.VMEM((steps, 2, edge, gates), BF16),
        pltpu.VMEM((steps, cols, gates), BF16),
        pltpu.VMEM((rows + 2, 2 * cols, 2 * cols), BF16),
        pltpu.VMEM((3 * width, 3 * gates), BF16),
        pltpu.VMEM((2 * edge, rows * cols), BF16),
        pltpu.VMEM((3 * width, padded), F32),
        pltpu.VMEM((3 * gates, 3 * width), F32),
        pltpu.VMEM((gates, taps + lanes + 128), F32),
        pltpu.VMEM((2, ncol, half, high, lanes), F32),
        pltpu.VMEM((2, ncol, half, high, lanes), BF16),
        pltpu.VMEM((ncol, half, high, lanes), BF16),
        pltpu.VMEM((ncol, half, high, lanes), F32),
        pltpu.VMEM((ncol, half, high, lanes), BF16),
        pltpu.VMEM((ncol - 1, half, high, lanes), BF16),
        pltpu.VMEM((half, high, lanes), F32),
        pltpu.VMEM((half, high, lanes), BF16),
        pltpu.VMEM((slots, high, lanes), BF16),
        pltpu.SemaphoreType.DMA((steps, len(SIDES))),
        pltpu.SemaphoreType.DMA((steps, len(SIDES))),
        pltpu.SemaphoreType.DMA((ncol + half,)),
        pltpu.SemaphoreType.DMA((ncol + half,)),
    ]
    each = high // ncol
    shapes = (
        jax.ShapeDtypeStruct(inputs.shape, BF16),
        jax.ShapeDtypeStruct(plane, F32),
        jax.ShapeDtypeStruct(plane, F32),
        jax.ShapeDtypeStruct((high, part), F32),
        jax.ShapeDtypeStruct((1, each), F32),
    )
    scratch += [pltpu.VMEM(shape.shape, shape.dtype) for shape in shapes]
    scratch.append(pltpu.SemaphoreType.DMA((steps + 4,)))
    hbm = pl.BlockSpec(memory_space=pltpu.HBM)
    results = pl.pallas_call(
        functools.partial(body, (steps, cin, hidden, rows, cols, nrow, ncol)),
        out_shape=shapes,
        in_specs=[hbm] * 7,
        out_specs=[hbm] * 5,
        scratch_shapes=scratch,
        compiler_params=pltpu.CompilerParams(
            collective_id=0, has_side_effects=True, vmem_limit_bytes=60 * 1024 * 1024
        ),
        name="convlstm_backward",
    )(inputs, gate_pre, cotangent, hidden_init, cell_init, land_mask, kernel)
    gin, gh, gc, gk, bias = pl.pallas_call(
        finish,
        out_shape=shapes,
        in_specs=[hbm] * 5,
        out_specs=[hbm] * 5,
        scratch_shapes=[pltpu.SemaphoreType.DMA((5,))],
        compiler_params=pltpu.CompilerParams(vmem_limit_bytes=60 * 1024 * 1024),
        name="write_outputs",
    )(*results)
    return gin, gh, gc, gk, bias.reshape(each)


def solution(mesh):
    placed = (
        P(None, None, "row", "col"),
        P(None, None, "row", "col"),
        P(None, None, "row", "col"),
        P(None, "row", "col"),
        P(None, "row", "col"),
        P("row", "col"),
        P(),
    )
    return jax.shard_map(
        functools.partial(shards, mesh.shape["row"], mesh.shape["col"]),
        mesh=mesh,
        in_specs=placed,
        out_specs=(
            P(None, None, "row", "col"),
            P(None, "row", "col"),
            P(None, "row", "col"),
            P("row", "col"),
            P(("row", "col")),
        ),
        check_vma=False,
    )
```

time: 261 us -> 69.4 us (0.27)
  local copies, waits for them, and re-layouts: 98.9 us -> 0 us
  Pallas kernels: 0 us -> 68.6 us
  starting transfers between devices: 45.6 us -> 0 us
  matrix products: 28.6 us -> 0 us
  blocking collectives: 25.8 us -> 0 us
  other arithmetic: 21.7 us -> 0 us
  waiting for transfers between devices: 21.7 us -> 0 us
  between operations: 16.9 us -> 0.64 us
    pallas_call x0 -> x2, Pallas kernels: none -> 68.6 us  [the longest x1 38.2 us: shards(): pl.pallas_call(functools.partial(body, (steps, cin, hidden, rows, cols, n...]
    slice x48 -> x0, local copies, waits for them, and re-layouts: 60.2 us -> none  [the longest x30 40.4 us: transposed(): padded_grads[:, 2 - upper:2 - upper + rows, 2 - left:2 - left + cols]]
    ppermute x16 -> x0, starting transfers between devices: 45.5 us -> none  [the longest x8 35.2 us: with_halo(): lax.ppermute(lax.slice_in_dim(block, block.shape[dim] - width, None, axis...]
    dot_general x54 -> x0, matrix products: 28.6 us -> none  [the longest x27 20 us: transposed(): lax.dot_general(piece, window, (((0,), (0,)), ((), ())), preferred_elemen...]
    unnamed x2 -> x0, blocking collectives: 25.8 us -> none
    reduce_scatter x1 -> x0, waiting for transfers between devices: 21.6 us -> none  [reduce_grads(): lax.psum_scatter(row_kernel, 'col', scatter_dimension=1, tiled=True)]
    unnamed x156 -> x0, local copies, waits for them, and re-layouts: 18.8 us -> none
    concatenate x11 -> x0, other arithmetic: 15.7 us -> none  [with_halo(): block = jnp.concatenate([low, block, high], axis=dim)]
  transfers between devices with their start and end apart: 18 -> 0, of which waited for: 1 -> 0; matrix products, arithmetic and copies ran while one was open for 39% -> 0% of each run, Pallas kernels for 0% -> 0%
where the time goes in v1:
time: 69.4 us; the launch traced here: 69.3 us
  Pallas kernels  68.6 us (99%)
    pallas_call x1, Pallas kernels, shards(): pl.pallas_call(functools.partial(body, (steps, cin, hidden, rows, cols, n...  38.2 us
    pallas_call x1, Pallas kernels, shards(): pl.pallas_call(finish, out_shape=shapes, in_specs=[hbm] * 5, out_specs=[h...  30.4 us

profile of v1, /device:TPU:0, one launch (start us, length us, event | category | flops | bytes accessed | tf_op | source)
XLA Modules:
  0.0 69.3 jit_solution(7899636073668806532)
XLA Ops:
  0.6 38.2 %convlstm_backward.1 = (bf16[3,64,8,128]{3,2,1,0:T(8,128)(2,1)}, f32[64,8,128]{2,1,0:T(8,128)}, f32[64,8,128]{2,1,0:T(8,128)}, f32[32,288]{1,0:T(8,128)}, f32[1,8]{1,0:T(1,128)}) custom-call(bf16[3,64,8,128]{3,2,1,0:T(8,128)(2,1)} %inp_in.1, bf16[3,256,8,128]{3,2,1,0:T(8,128)(2,1)} %pre_in.1, bf16[3,64,8,128]{3,2,1,0:T(8,128)(2,1)} %cot_in.1, ...), custom_call_target="tpu_custom_call" | custom-call | tf_op jit(solution)/shard_map/convlstm_backward/pallas_call | solution.py:468
  38.8 30.4 %write_outputs.1 = (bf16[3,64,8,128]{3,2,1,0:T(8,128)(2,1)}, f32[64,8,128]{2,1,0:T(8,128)}, f32[64,8,128]{2,1,0:T(8,128)}, f32[32,288]{1,0:T(8,128)}, f32[1,8]{1,0:T(1,128)}) custom-call(bf16[3,64,8,128]{3,2,1,0:T(8,128)(2,1)} %get-tuple-element.15.refs_0_, f32[64,8,128]{2,1,0:T(8,128)} %get-tuple-element.16.refs_1_, ...), custom_call_target="tpu_custom_call" | custom-call | tf_op jit(solution)/shard_map/write_outputs/pallas_call | solution.py:479

commit v2 on v1

--- a/solution.py
+++ b/solution.py
@@ -396,11 +396,16 @@
 
 def finish(*refs):
     sem = refs[-1]
-    count = (len(refs) - 1) // 2
-    copies = [pltpu.make_async_copy(refs[n], refs[count + n], sem.at[n]) for n in range(count)]
-    for copy in copies:
+    count = (len(refs) - 1) // 3
+    sources, targets, held = refs[:count], refs[count : 2 * count], refs[2 * count : 3 * count]
+    reads = [pltpu.make_async_copy(sources[n], held[n], sem.at[n]) for n in range(count)]
+    writes = [pltpu.make_async_copy(held[n], targets[n], sem.at[count + n]) for n in range(count)]
+    for copy in reads:
         copy.start()
-    for copy in copies:
+    for n in range(count):
+        reads[n].wait()
+        writes[n].start()
+    for copy in writes:
         copy.wait()
 
 
@@ -481,7 +486,7 @@
         out_shape=shapes,
         in_specs=[hbm] * 5,
         out_specs=[hbm] * 5,
-        scratch_shapes=[pltpu.SemaphoreType.DMA((5,))],
+        scratch_shapes=[pltpu.VMEM(shape.shape, shape.dtype) for shape in shapes] + [pltpu.SemaphoreType.DMA((10,))],
         compiler_params=pltpu.CompilerParams(vmem_limit_bytes=60 * 1024 * 1024),
         name="write_outputs",
     )(*results)

time: 69.4 us -> 41 us (0.59)
  Pallas kernels: 68.6 us -> 40.2 us
    pallas_call x1, Pallas kernels: 30.4 us -> 2.01 us  [shards(): pl.pallas_call(finish, out_shape=shapes, in_specs=[hbm] * 5, out_specs=[h...]
where the time goes in v2:
time: 41 us; the launch traced here: 40.8 us
  Pallas kernels  40.2 us (98%)
  between operations  0.64 us (2%)
    pallas_call x1, Pallas kernels, shards(): pl.pallas_call(functools.partial(body, (steps, cin, hidden, rows, cols, n...  38.2 us
    pallas_call x1, Pallas kernels, shards(): pl.pallas_call(finish, out_shape=shapes, in_specs=[hbm] * 5, out_specs=[h...  2.01 us

profile of v2, /device:TPU:0, one launch (start us, length us, event | category | flops | bytes accessed | tf_op | source)
XLA Modules:
  0.0 40.8 jit_solution(4164753133265615858)
XLA Ops:
  0.6 38.2 %convlstm_backward.1 = (bf16[3,64,8,128]{3,2,1,0:T(8,128)(2,1)}, f32[64,8,128]{2,1,0:T(8,128)}, f32[64,8,128]{2,1,0:T(8,128)}, f32[32,288]{1,0:T(8,128)}, f32[1,8]{1,0:T(1,128)}) custom-call(bf16[3,64,8,128]{3,2,1,0:T(8,128)(2,1)} %inp_in.1, bf16[3,256,8,128]{3,2,1,0:T(8,128)(2,1)} %pre_in.1, bf16[3,64,8,128]{3,2,1,0:T(8,128)(2,1)} %cot_in.1, ...), custom_call_target="tpu_custom_call" | custom-call | tf_op jit(solution)/shard_map/convlstm_backward/pallas_call | solution.py:473
  38.8 2.0 %write_outputs.1 = (bf16[3,64,8,128]{3,2,1,0:T(8,128)(2,1)}, f32[64,8,128]{2,1,0:T(8,128)}, f32[64,8,128]{2,1,0:T(8,128)}, f32[32,288]{1,0:T(8,128)}, f32[1,8]{1,0:T(1,128)}) custom-call(bf16[3,64,8,128]{3,2,1,0:T(8,128)(2,1)} %get-tuple-element.15.refs_0_, f32[64,8,128]{2,1,0:T(8,128)} %get-tuple-element.16.refs_1_, ...), custom_call_target="tpu_custom_call" | custom-call | tf_op jit(solution)/shard_map/write_outputs/pallas_call | solution.py:484

commit v3 on v2

--- a/solution.py
+++ b/solution.py
@@ -32,8 +32,8 @@
     inp_in, pre_in, cot_in, hid_in, cell_in, mask_in, weight_in,
     gin_hbm, gh_hbm, gc_hbm, gk_hbm, bias_hbm,
     inp, pre, cot, hid, cell, mask, weight, load_sem,
-    acts, cells, tanhs, gradc, nat, zst, aall, edges, border, shifter, weight_t, selector,
-    product, kacc, kfull, kown, kbuf, r1, s1own, s1, r2, s2own, s2, r3,
+    acts, cells, tanhs, gradc, nat, zwin, zedges, zborder, aall, edges, border, shifter, colsel, weight_t, selector,
+    product, ymain, kfull, kown, kbuf, r1, s1own, s1, r2, s2own, s2, r3,
     send_sem, recv_sem, rs_send, rs_recv,
     gin_out, gh_out, gc_out, gk_out, bias_out, store_sem,
 ):
@@ -65,6 +65,9 @@
     for step in range(steps):
         aall[step, gates : 2 * gates, 0:cols] = jnp.zeros((gates, cols), BF16)
         aall[step, gates : 2 * gates, padded - cols : padded] = jnp.zeros((gates, cols), BF16)
+        zwin[step, width : 2 * width, 0:cols] = jnp.zeros((width, cols), BF16)
+        zwin[step, width : 2 * width, padded - cols : padded] = jnp.zeros((width, cols), BF16)
+    zborder[...] = jnp.zeros_like(zborder)
 
     barrier = pltpu.get_barrier_semaphore()
     for dr, dc in SIDES:
@@ -98,8 +101,19 @@
     wanted = jnp.where(prow < edge, prow * cols, (prow - edge) * cols + cols - 1)
     valid = (prow % edge) < rows
     selector[...] = ((pcol == wanted) & valid).astype(F32).astype(BF16)
-    irow = lax.broadcasted_iota(jnp.int32, (gates, gates), 0)
-    icol = lax.broadcasted_iota(jnp.int32, (gates, gates), 1)
+    gap = cols // rows
+    crow = lax.broadcasted_iota(jnp.int32, (cols, cols), 0)
+    ccol = lax.broadcasted_iota(jnp.int32, (cols, cols), 1)
+    for side in range(2):
+        at = crow if side == 0 else (crow + 1) % cols
+        for dr in range(3):
+            j = at // gap + 2 - dr
+            near = side * 3 * edge
+            source = jnp.where(j == 0, near + edge + rows - 1, jnp.where(j == rows + 1, near + 2 * edge, near + j - 1))
+            n = side * 3 + dr
+            colsel[n * cols : (n + 1) * cols] = ((ccol == source) & (at % gap == 0)).astype(F32).astype(BF16)
+    irow = lax.broadcasted_iota(jnp.int32, (width, width), 0)
+    icol = lax.broadcasted_iota(jnp.int32, (width, width), 1)
     identity = (irow == icol).astype(F32).astype(BF16)
 
     loads[0].wait()
@@ -112,15 +126,7 @@
     def place_z(step, first, count):
         for r in range(rows):
             tile = nat[pl.ds(r, count, stride=rows), :].astype(BF16)
-            for dr in range(3):
-                at = (r + 2 - dr) * cols
-                zst[step, dr * width + first : dr * width + first + count, at : at + cols] = tile
-
-    for step in range(steps):
-        for dr in range(3):
-            for i in range(rows + 2):
-                if not 0 <= i + dr - 2 < rows:
-                    zst[step, dr * width : (dr + 1) * width, i * cols : (i + 1) * cols] = jnp.zeros((width, cols), BF16)
+            zwin[step, width + first : width + first + count, (r + 1) * cols : (r + 2) * cols] = tile
 
     def spread(ref, step=None):
         def put(b, carry):
@@ -157,7 +163,15 @@
 
     def halo(step, d):
         dr, dc = SIDES[d]
-        if dc == 0:
+        if dc == 0 and step == steps:
+            first = cols if dr < 0 else rows * cols
+            land_at = padded - cols if dr < 0 else 0
+            src = zwin.at[:, pl.ds(width, width), pl.ds(first, cols)]
+            dst = zwin.at[:, pl.ds(width, width), pl.ds(land_at, cols)]
+        elif step == steps:
+            src = zedges.at[1 if dc > 0 else 0]
+            dst = zborder.at[pl.ds((d - 2) * edge, edge)]
+        elif dc == 0:
             first = cols if dr < 0 else rows * cols
             land_at = padded - cols if dr < 0 else 0
             src = aall.at[step, pl.ds(gates, gates), pl.ds(first, cols)]
@@ -189,8 +203,29 @@
                 halo(step, d).wait_send()
 
     def kernel_terms(step):
-        term = nt(aall[step], zst[step])
-        kacc[...] = term if step == steps - 1 else kacc[...] + term
+        own = aall[step, gates : 2 * gates, cols : padded - cols]
+        for dr in range(3):
+            at = slice(dr * 3 * width, (dr + 1) * 3 * width)
+            term = nt(own, zwin[step, :, dr * cols : (dr + rows) * cols])
+            kfull[:, at] = term if step == steps - 1 else kfull[:, at] + term
+
+    def z_edges():
+        for s in range(steps):
+            picked = nt(selector[...], zwin[s, width : 2 * width, cols : padded - cols]).astype(BF16)
+            zedges[0, :, s * width : (s + 1) * width] = picked[:edge]
+            zedges[1, :, s * width : (s + 1) * width] = picked[edge:]
+
+    def z_windows():
+        sides = [nt(identity, zborder[:, s * width : (s + 1) * width]).astype(BF16) for s in range(steps)]
+        for j in range(rows + 2):
+            at = slice(j * cols, (j + 1) * cols)
+            pairs = jnp.concatenate(
+                [jnp.concatenate([zwin[s, width : 2 * width, at], sides[s]], axis=1) for s in range(steps)], axis=0
+            )
+            moved = nn(pairs, shifter[j]).astype(BF16)
+            for s in range(steps):
+                zwin[s, 0:width, at] = moved[s * width : (s + 1) * width, :cols]
+                zwin[s, 2 * width : 3 * width, at] = moved[s * width : (s + 1) * width, cols:]
 
     def emit_inputs(step):
         def put(b, carry):
@@ -202,18 +237,49 @@
         store.start()
         stores.append(store)
 
-    def transposed(step):
-        product[...] = nn(weight_t[...], aall[step])
+    def shift_row(step, j):
+        at = slice(j * cols, (j + 1) * cols)
+        moved = nn(aall[step, gates : 2 * gates, at], shifter[1, :cols]).astype(BF16)
+        aall[step, 2 * gates : 3 * gates, at] = moved[:, :cols]
+        aall[step, 0:gates, at] = moved[:, cols:]
+
+    def transposed_own(step):
+        for r in range(rows):
+            shift_row(step, r + 1)
+        product[...] = nn(weight_t[...], aall[step, :, cols : padded - cols])
         for r in range(rows):
             total = None
             for dr in range(3):
-                at = (r + 2 - dr) * cols
-                piece = product[dr * width : (dr + 1) * width, at : at + cols]
-                total = piece if total is None else total + piece
-            gxn = pl.ds(gates * rows + r, cin, stride=rows)
-            nat[gxn, :] = total[:cin]
-            dhn = pl.ds((gates + cin) * rows + r, hidden, stride=rows)
-            nat[dhn, :] = total[cin:]
+                if 0 <= r + 1 - dr < rows:
+                    at = (r + 1 - dr) * cols
+                    piece = product[dr * width : (dr + 1) * width, at : at + cols]
+                    total = piece if total is None else total + piece
+            ymain[:, r * cols : (r + 1) * cols] = total
+
+    def transposed_halo(step):
+        shift_row(step, 0)
+        shift_row(step, rows + 1)
+        above = nn(weight_t[2 * width : 3 * width], aall[step, :, 0:cols])
+        below = nn(weight_t[0:width], aall[step, :, padded - cols : padded])
+        picked = nn(colsel[...], border[step]).astype(BF16)
+        sides = None
+        for side in range(2):
+            for dr in range(3):
+                n, k = side * 3 + dr, 3 * dr + 2 - 2 * side
+                piece = nn(picked[n * cols : (n + 1) * cols], weight[:, k * width : (k + 1) * width])
+                sides = piece if sides is None else sides + piece
+        sides = sides.T
+        lane = lax.broadcasted_iota(jnp.int32, (width, cols), 1)
+        outer = (lane == 0) | (lane == cols - 1)
+        for r in range(rows):
+            moved = pltpu.roll(sides, cols - gap * r, 1) if r else sides
+            total = ymain[:, r * cols : (r + 1) * cols] + jnp.where(outer, moved, 0.0)
+            if r == 0:
+                total = total + above
+            if r == rows - 1:
+                total = total + below
+            nat[pl.ds(gates * rows + r, cin, stride=rows), :] = total[:cin]
+            nat[pl.ds((gates + cin) * rows + r, hidden, stride=rows), :] = total[cin:]
 
     bias = None
     stores = []
@@ -261,6 +327,7 @@
                     weight_t[dr * width : (dr + 1) * width, dc * gates : (dc + 1) * gates] = (
                         weight[:, k * width : (k + 1) * width].astype(F32).T.astype(BF16)
                     )
+            transposed_own(step)
             loads[steps + 4].wait()
             loads[steps + 5].wait()
             spread(hid)
@@ -268,26 +335,22 @@
             for s in range(steps):
                 spread(inp, s)
                 place_z(s, 0, cin)
+            z_edges()
+            start_halo(steps)
+        elif step > 0:
+            transposed_own(step)
+            emit_inputs(step + 1)
+            if step == steps - 2:
+                wait_halo(steps)
+                z_windows()
+                kernel_terms(steps - 1)
+            kernel_terms(step)
         else:
-            emit_inputs(step + 1)
-            kernel_terms(step + 1)
-        wait_halo(step)
-        side = nt(identity, border[step]).astype(BF16)
-        for j in range(rows + 2):
-            at = slice(j * cols, (j + 1) * cols)
-            pair = jnp.concatenate([aall[step, gates : 2 * gates, at], side], axis=1)
-            moved = nn(pair, shifter[j]).astype(BF16)
-            aall[step, 2 * gates : 3 * gates, at] = moved[:, :cols]
-            aall[step, 0:gates, at] = moved[:, cols:]
+            kernel_terms(0)
         if step > 0:
-            transposed(step)
-        wait_sent(step)
-
-    kernel_terms(0)
-    for dr in range(3):
-        for dc in range(3):
-            k = 3 * dr + dc
-            kfull[:, k * width : (k + 1) * width] = kacc[dc * gates : (dc + 1) * gates, dr * width : (dr + 1) * width] * scale
+            wait_halo(step)
+            transposed_halo(step)
+
     lane = lax.broadcasted_iota(jnp.int32, (gates, lanes), 1)
     tail = lanes - 128
 
@@ -312,7 +375,7 @@
         piece = kfull[:, base : base + lanes + 128]
         if shift:
             piece = pltpu.roll(piece, lanes + 128 - shift, 1)
-        piece = jnp.where(lane < part, piece[:, :lanes], jnp.where(lane == part, bias, 0.0))
+        piece = jnp.where(lane < part, piece[:, :lanes] * scale, jnp.where(lane == part, bias, 0.0))
         sent = split(piece)[1]
         for r in range(nrow):
             kown[r % 2, c, r // 2] = piece[r * high : (r + 1) * high]
@@ -339,7 +402,11 @@
         )
 
     first().start()
-    transposed(0)
+    transposed_own(0)
+    if steps > 1:
+        emit_inputs(1)
+    wait_halo(0)
+    transposed_halo(0)
     first().wait_recv()
     for c in range(ncol):
         for z in range(half):
@@ -380,6 +447,8 @@
         stores.append(store)
     for store in stores:
         store.wait()
+    for step in range(steps + 1):
+        wait_sent(step)
     first().wait_send()
     for j in range(1, ncol):
         second(j).wait_send()
@@ -436,14 +505,17 @@
         pltpu.VMEM(plane, F32),
         pltpu.VMEM(((gates + width) * rows, cols), F32),
         pltpu.VMEM((steps, 3 * width, padded), BF16),
+        pltpu.VMEM((2, edge, steps * width), BF16),
+        pltpu.VMEM((cols, steps * width), BF16),
         pltpu.VMEM((steps, 3 * gates, padded), BF16),
         pltpu.VMEM((steps, 2, edge, gates), BF16),
         pltpu.VMEM((steps, cols, gates), BF16),
         pltpu.VMEM((rows + 2, 2 * cols, 2 * cols), BF16),
+        pltpu.VMEM((6 * cols, cols), BF16),
         pltpu.VMEM((3 * width, 3 * gates), BF16),
         pltpu.VMEM((2 * edge, rows * cols), BF16),
-        pltpu.VMEM((3 * width, padded), F32),
-        pltpu.VMEM((3 * gates, 3 * width), F32),
+        pltpu.VMEM((3 * width, rows * cols), F32),
+        pltpu.VMEM((width, rows * cols), F32),
         pltpu.VMEM((gates, taps + lanes + 128), F32),
         pltpu.VMEM((2, ncol, half, high, lanes), F32),
         pltpu.VMEM((2, ncol, half, high, lanes), BF16),
@@ -454,8 +526,8 @@
         pltpu.VMEM((half, high, lanes), F32),
         pltpu.VMEM((half, high, lanes), BF16),
         pltpu.VMEM((slots, high, lanes), BF16),
-        pltpu.SemaphoreType.DMA((steps, len(SIDES))),
-        pltpu.SemaphoreType.DMA((steps, len(SIDES))),
+        pltpu.SemaphoreType.DMA((steps + 1, len(SIDES))),
+        pltpu.SemaphoreType.DMA((steps + 1, len(SIDES))),
         pltpu.SemaphoreType.DMA((ncol + half,)),
         pltpu.SemaphoreType.DMA((ncol + half,)),
     ]

time: 41 us -> 37.2 us (0.907)
  Pallas kernels: 40.2 us -> 36.4 us
    pallas_call x1, Pallas kernels: 38.2 us -> 34.4 us  [shards(): pl.pallas_call(functools.partial(body, (steps, cin, hidden, rows, cols, n...]
where the time goes in v3:
time: 37.2 us; the launch traced here: 37.1 us
  Pallas kernels  36.4 us (98%)
  between operations  0.64 us (2%)
    pallas_call x1, Pallas kernels, shards(): pl.pallas_call(functools.partial(body, (steps, cin, hidden, rows, cols, n...  34.4 us
    pallas_call x1, Pallas kernels, shards(): pl.pallas_call(finish, out_shape=shapes, in_specs=[hbm] * 5, out_specs=[h...  2.01 us

profile of v3, /device:TPU:0, one launch (start us, length us, event | category | flops | bytes accessed | tf_op | source)
XLA Modules:
  0.0 37.1 jit_solution(14644153055036627225)
XLA Ops:
  0.6 34.4 %convlstm_backward.1 = (bf16[3,64,8,128]{3,2,1,0:T(8,128)(2,1)}, f32[64,8,128]{2,1,0:T(8,128)}, f32[64,8,128]{2,1,0:T(8,128)}, f32[32,288]{1,0:T(8,128)}, f32[1,8]{1,0:T(1,128)}) custom-call(bf16[3,64,8,128]{3,2,1,0:T(8,128)(2,1)} %inp_in.1, bf16[3,256,8,128]{3,2,1,0:T(8,128)(2,1)} %pre_in.1, bf16[3,64,8,128]{3,2,1,0:T(8,128)(2,1)} %cot_in.1, ...), custom_call_target="tpu_custom_call" | custom-call | tf_op jit(solution)/shard_map/convlstm_backward/pallas_call | solution.py:545
  35.1 2.0 %write_outputs.1 = (bf16[3,64,8,128]{3,2,1,0:T(8,128)(2,1)}, f32[64,8,128]{2,1,0:T(8,128)}, f32[64,8,128]{2,1,0:T(8,128)}, f32[32,288]{1,0:T(8,128)}, f32[1,8]{1,0:T(1,128)}) custom-call(bf16[3,64,8,128]{3,2,1,0:T(8,128)(2,1)} %get-tuple-element.15.refs_0_, f32[64,8,128]{2,1,0:T(8,128)} %get-tuple-element.16.refs_1_, ...), custom_call_target="tpu_custom_call" | custom-call | tf_op jit(solution)/shard_map/write_outputs/pallas_call | solution.py:556

commit v4 on v3

--- a/solution.py
+++ b/solution.py
@@ -34,7 +34,7 @@
     inp, pre, cot, hid, cell, mask, weight, load_sem,
     acts, cells, tanhs, gradc, nat, zwin, zedges, zborder, aall, edges, border, shifter, colsel, weight_t, selector,
     product, ymain, kfull, kown, kbuf, r1, s1own, s1, r2, s2own, s2, r3,
-    send_sem, recv_sem, rs_send, rs_recv,
+    send_sem, recv_sem, one_send, one_recv, two_send, two_recv, three_send, three_recv,
     gin_out, gh_out, gc_out, gk_out, bias_out, store_sem,
 ):
     steps, cin, hidden, rows, cols, nrow, ncol = dims
@@ -369,6 +369,20 @@
             jnp.concatenate([rest.astype(BF16), sent], axis=-1),
         )
 
+    def first(c):
+        return pltpu.make_async_remote_copy(
+            src_ref=kbuf.at[1 - core, c], dst_ref=r1.at[c], send_sem=one_send.at[c], recv_sem=one_recv.at[c],
+            device_id=(sibling, col), device_id_type=MESH,
+        )
+
+    def second(j, z):
+        to = (col + j) % ncol
+        return pltpu.make_async_remote_copy(
+            src_ref=s1.at[to, z], dst_ref=r2.at[j - 1, z],
+            send_sem=two_send.at[j - 1, z], recv_sem=two_recv.at[j - 1, z],
+            device_id=(row, to), device_id_type=MESH,
+        )
+
     bias = jnp.sum(bias, axis=1, keepdims=True) * scale
     for c in range(ncol):
         base, shift = part * c // 128 * 128, part * c % 128
@@ -380,39 +394,28 @@
         for r in range(nrow):
             kown[r % 2, c, r // 2] = piece[r * high : (r + 1) * high]
             kbuf[r % 2, c, r // 2] = sent[r * high : (r + 1) * high]
-
-    def first():
-        return pltpu.make_async_remote_copy(
-            src_ref=kbuf.at[1 - core], dst_ref=r1, send_sem=rs_send.at[0], recv_sem=rs_recv.at[0],
-            device_id=(sibling, col), device_id_type=MESH,
-        )
-
-    def second(j):
-        to = (col + j) % ncol
-        return pltpu.make_async_remote_copy(
-            src_ref=s1.at[to], dst_ref=r2.at[j - 1], send_sem=rs_send.at[j], recv_sem=rs_recv.at[j],
-            device_id=(row, to), device_id_type=MESH,
-        )
+        first(c).start()
 
     def third(j):
         to = (zpos + j) % half
         return pltpu.make_async_remote_copy(
-            src_ref=s2.at[to], dst_ref=r3.at[j - 1], send_sem=rs_send.at[ncol + j], recv_sem=rs_recv.at[ncol + j],
+            src_ref=s2.at[to], dst_ref=r3.at[j - 1], send_sem=three_send.at[j], recv_sem=three_recv.at[j],
             device_id=(to * 2 + core, col), device_id_type=MESH,
         )
 
-    first().start()
     transposed_own(0)
+    order = [(zpos + j) % half for j in (*range(1, half), 0)]
+    for j in (*range(1, ncol), 0):
+        c = (col + j) % ncol
+        first(c).wait_recv()
+        for z in order:
+            s1own[c, z], s1[c, z] = split(kown[core, c, z] + r1[c, z].astype(F32))
+            if j:
+                second(j, z).start()
     if steps > 1:
         emit_inputs(1)
     wait_halo(0)
     transposed_halo(0)
-    first().wait_recv()
-    for c in range(ncol):
-        for z in range(half):
-            s1own[c, z], s1[c, z] = split(kown[core, c, z] + r1[c, z].astype(F32))
-    for j in range(1, ncol):
-        second(j).start()
     emit_inputs(0)
     gh_out[...] = nat[pl.ds((gates + cin) * rows, hidden * rows), :].reshape(hidden, rows, cols)
     gc_out[...] = gradc[...]
@@ -420,15 +423,14 @@
         store = pltpu.make_async_copy(source, target, store_sem.at[steps + n])
         store.start()
         stores.append(store)
-    for j in range(1, ncol):
-        second(j).wait_recv()
-    for z in range(half):
+    for n, z in enumerate(order):
         total = s1own[col, z]
         for j in range(1, ncol):
+            second(j, z).wait_recv()
             total = total + r2[j - 1, z].astype(F32)
         s2own[z], s2[z] = split(total)
-    for j in range(1, half):
-        third(j).start()
+        if n + 1 < half:
+            third(n + 1).start()
     total = s2own[zpos]
     for j in range(1, half):
         third(j).wait_recv()
@@ -449,9 +451,11 @@
         store.wait()
     for step in range(steps + 1):
         wait_sent(step)
-    first().wait_send()
+    for c in range(ncol):
+        first(c).wait_send()
     for j in range(1, ncol):
-        second(j).wait_send()
+        for z in range(half):
+            second(j, z).wait_send()
     for j in range(1, half):
         third(j).wait_send()
 
@@ -528,8 +532,12 @@
         pltpu.VMEM((slots, high, lanes), BF16),
         pltpu.SemaphoreType.DMA((steps + 1, len(SIDES))),
         pltpu.SemaphoreType.DMA((steps + 1, len(SIDES))),
-        pltpu.SemaphoreType.DMA((ncol + half,)),
-        pltpu.SemaphoreType.DMA((ncol + half,)),
+        pltpu.SemaphoreType.DMA((ncol,)),
+        pltpu.SemaphoreType.DMA((ncol,)),
+        pltpu.SemaphoreType.DMA((ncol - 1, half)),
+        pltpu.SemaphoreType.DMA((ncol - 1, half)),
+        pltpu.SemaphoreType.DMA((half,)),
+        pltpu.SemaphoreType.DMA((half,)),
     ]
     each = high // ncol
     shapes = (

time: 37.2 us -> 34.8 us (0.935)
  Pallas kernels: 36.4 us -> 34 us
    pallas_call x1, Pallas kernels: 34.4 us -> 32 us  [shards(): pl.pallas_call(functools.partial(body, (steps, cin, hidden, rows, cols, n...]
where the time goes in v4:
time: 34.8 us; the launch traced here: 34.6 us
  Pallas kernels  34 us (98%)
  between operations  0.64 us (2%)
    pallas_call x1, Pallas kernels, shards(): pl.pallas_call(functools.partial(body, (steps, cin, hidden, rows, cols, n...  32 us
    pallas_call x1, Pallas kernels, shards(): pl.pallas_call(finish, out_shape=shapes, in_specs=[hbm] * 5, out_specs=[h...  2.01 us

profile of v4, /device:TPU:0, one launch (start us, length us, event | category | flops | bytes accessed | tf_op | source)
XLA Modules:
  0.0 34.6 jit_solution(15680908068708573857)
XLA Ops:
  0.6 32.0 %convlstm_backward.1 = (bf16[3,64,8,128]{3,2,1,0:T(8,128)(2,1)}, f32[64,8,128]{2,1,0:T(8,128)}, f32[64,8,128]{2,1,0:T(8,128)}, f32[32,288]{1,0:T(8,128)}, f32[1,8]{1,0:T(1,128)}) custom-call(bf16[3,64,8,128]{3,2,1,0:T(8,128)(2,1)} %inp_in.1, bf16[3,256,8,128]{3,2,1,0:T(8,128)(2,1)} %pre_in.1, bf16[3,64,8,128]{3,2,1,0:T(8,128)(2,1)} %cot_in.1, ...), custom_call_target="tpu_custom_call" | custom-call | tf_op jit(solution)/shard_map/convlstm_backward/pallas_call | solution.py:553
  32.6 2.0 %write_outputs.1 = (bf16[3,64,8,128]{3,2,1,0:T(8,128)(2,1)}, f32[64,8,128]{2,1,0:T(8,128)}, f32[64,8,128]{2,1,0:T(8,128)}, f32[32,288]{1,0:T(8,128)}, f32[1,8]{1,0:T(1,128)}) custom-call(bf16[3,64,8,128]{3,2,1,0:T(8,128)(2,1)} %get-tuple-element.15.refs_0_, f32[64,8,128]{2,1,0:T(8,128)} %get-tuple-element.16.refs_1_, ...), custom_call_target="tpu_custom_call" | custom-call | tf_op jit(solution)/shard_map/write_outputs/pallas_call | solution.py:564
